TPU v7x, 32 devices: a whole 2x2x4 slice. The times are simulated.
32 devices in a mesh: groups: 2 (over x), seq: 16 (over z, y, core).
Axes of the slice: x: 2, y: 2, z: 4, core: 2. Of those that a mesh axis runs over, the one named last changes fastest.
Arguments:
- tokens: bfloat16 [8192, 256], P(('groups', 'seq')), parts along dimension 0, may hold values from -6 to 6
- norm_gain: float32 [256], replicated, may hold values from 0.1 to 1.9
- w_in: bfloat16 [256, 768], replicated, may hold values from -0.375 to 0.375
- short_filter: float32 [3, 768], replicated, may hold values from -0.8 to 0.8
- long_filter: float32 [4096, 256], P('seq'), may hold values from -0.09375 to 0.09375
- medium_filter: float32 [128, 256], replicated, may hold values from -0.5 to 0.5
- skip_gain: float32 [256], replicated, may hold values from -1 to 1
- w_out: bfloat16 [256, 256], replicated, may hold values from -0.375 to 0.375
Outputs:
- result: bfloat16 [8192, 256], P(('groups', 'seq')), parts along dimension 0
There are 2 independent parts, one for each index of `groups`. A program takes and returns all parts, laid end to end along the dimension named above; an argument that names none is the same for every part. Nothing has to cross between parts.
All inputs are finite; a program needn't handle non-finite values.
Results may differ from a plain program's by a relative error of at most 0.015.
Values may be sent and summed in bfloat16 or wider, within the bound.
No kernel may reach another device: no remote copies, remote signals or barrier semaphores. Data moves between devices by JAX's collectives and lax.ppermute only.
A program may use at most 64 MiB of HBM per device.

v0:
```python
import math

import jax
import jax.numpy as jnp
from jax import lax
from jax.sharding import PartitionSpec as P

epsilon = 1e-06
highest = lax.Precision.HIGHEST


def from_behind(array, axis, by):
    devices = lax.axis_size(axis)
    pairs = [(i, i + by) for i in range(devices) if 0 <= i + by < devices]
    return lax.ppermute(array, axis, pairs)


def from_partner(array, axis, distance):
    return lax.ppermute(array, axis, [(i, i ^ 1 << distance) for i in range(lax.axis_size(axis))])


def reverse_bits(my_index, bit_count):
    flipped = jnp.zeros((), jnp.int32)
    for bit_num in range(bit_count):
        flipped = flipped + my_index // 2**bit_num % 2 * 2 ** (bit_count - 1 - bit_num)
    return flipped


def phase_table(first, second, modulus):
    products = first[:, None] * second[None, :] % modulus
    phase_angle = 2.0 * math.pi / modulus * products.astype(jnp.float32)
    return (jnp.cos(phase_angle), jnp.sin(phase_angle))


def spectral_middle(current, column, tok_rows, full_len):
    freq_one = 2 * column + jnp.arange(2, dtype=jnp.int32)
    offsets = jnp.arange(tok_rows, dtype=jnp.int32)
    tw_cos, tw_sin = phase_table(freq_one, offsets, full_len)
    tw_cos = tw_cos[:, :, None]
    tw_sin = tw_sin[:, :, None]
    real_part = current[0] * tw_cos + current[1] * tw_sin
    imag_part = current[1] * tw_cos - current[0] * tw_sin
    cos_table, sin_table = phase_table(offsets, offsets, tok_rows)
    spec_re = jnp.einsum("kt,setd->sekd", cos_table, real_part, precision=highest) + jnp.einsum(
        "kt,setd->sekd", sin_table, imag_part, precision=highest
    )
    spec_im = jnp.einsum("kt,setd->sekd", cos_table, imag_part, precision=highest) - jnp.einsum(
        "kt,setd->sekd", sin_table, real_part, precision=highest
    )
    prod_re = spec_re[0] * spec_re[1] - spec_im[0] * spec_im[1]
    prod_im = spec_re[0] * spec_im[1] + spec_im[0] * spec_re[1]
    back_re = jnp.einsum("tk,ekd->etd", cos_table, prod_re, precision=highest) - jnp.einsum(
        "tk,ekd->etd", sin_table, prod_im, precision=highest
    )
    back_im = jnp.einsum("tk,ekd->etd", cos_table, prod_im, precision=highest) + jnp.einsum(
        "tk,ekd->etd", sin_table, prod_re, precision=highest
    )
    return jnp.stack([back_re * tw_cos - back_im * tw_sin, back_re * tw_sin + back_im * tw_cos])


def local(tokens, norm_gain, w_in, short_filter, long_filter, medium_filter, skip_gain, w_out):
    tok_rows, chan_width = tokens.shape
    devices = lax.axis_size("seq")
    my_index = lax.axis_index("seq")
    full_len = 2 * tok_rows * devices
    inputs = tokens.astype(jnp.float32)
    mean_sq = jnp.mean(inputs * inputs, axis=-1, keepdims=True)
    normed = (inputs * lax.rsqrt(mean_sq + epsilon) * norm_gain).astype(jnp.bfloat16)
    projected = jnp.dot(normed, w_in, preferred_element_type=jnp.float32).astype(jnp.bfloat16)
    taps_count = short_filter.shape[0]
    rim_rows = from_behind(projected[tok_rows - (taps_count - 1) :], "seq", 1)
    extended = jnp.concatenate([rim_rows, projected], axis=0)
    short_mix = jnp.zeros((tok_rows, projected.shape[1]), jnp.float32)
    for tap_num in range(taps_count):
        begin = taps_count - 1 - tap_num
        short_mix = short_mix + short_filter[tap_num] * extended[begin : begin + tok_rows]
    query_part = short_mix[:, 0:chan_width]
    key_part = short_mix[:, chan_width : 2 * chan_width]
    value_part = short_mix[:, 2 * chan_width : 3 * chan_width]
    signal = key_part * value_part
    med_len = medium_filter.shape[0]
    med_rows = from_behind(
        signal[tok_rows - (med_len - 1) :].astype(jnp.bfloat16), "seq", 1
    ).astype(jnp.float32)
    med_ext = jnp.concatenate([med_rows, signal], axis=0)

    def add_group(group_num, acc):
        for inner in range(8):
            tap_num = group_num * 8 + inner
            weights = lax.dynamic_slice_in_dim(medium_filter, tap_num, 1, 0)
            window = lax.dynamic_slice_in_dim(med_ext, med_len - 1 - tap_num, tok_rows, 0)
            acc = acc + weights * window
        return acc

    med_out = lax.fori_loop(0, med_len // 8, add_group, jnp.zeros_like(signal))
    sig_pair = jnp.stack([signal, long_filter])
    bit_count = devices.bit_length() - 1
    start_phase = 2.0 * math.pi / (2 * devices) * my_index.astype(jnp.float32)
    real_part = jnp.stack([sig_pair, sig_pair * jnp.cos(start_phase)], axis=1)
    imag_part = jnp.stack([jnp.zeros_like(sig_pair), -sig_pair * jnp.sin(start_phase)], axis=1)
    current = jnp.stack([real_part, imag_part])
    for bit_num in reversed(range(bit_count)):
        half_span = 2**bit_num
        blk_span = 2 * half_span
        partner = from_partner(current.astype(jnp.bfloat16), "seq", bit_num).astype(current.dtype)
        is_upper = my_index // half_span % 2 == 1
        phase_angle = (
            2.0 * math.pi / blk_span * (my_index % blk_span - half_span).astype(jnp.float32)
        )
        summed = current + partner
        differ = partner - current
        w_real = jnp.cos(phase_angle)
        w_imag = -jnp.sin(phase_angle)
        upper_val = jnp.stack(
            [differ[0] * w_real - differ[1] * w_imag, differ[0] * w_imag + differ[1] * w_real]
        )
        current = jnp.where(is_upper, upper_val, summed)
    column = reverse_bits(my_index, bit_count)
    current = spectral_middle(current, column, tok_rows, full_len)
    for bit_num in range(bit_count):
        half_span = 2**bit_num
        blk_span = 2 * half_span
        partner = from_partner(current.astype(jnp.bfloat16), "seq", bit_num).astype(current.dtype)
        is_upper = my_index // half_span % 2 == 1
        inner_pos = my_index % blk_span - jnp.where(is_upper, half_span, 0)
        phase_angle = 2.0 * math.pi / blk_span * inner_pos.astype(jnp.float32)
        w_real = jnp.cos(phase_angle)
        w_imag = jnp.sin(phase_angle)
        factor = jnp.where(is_upper, current, partner)
        base_val = jnp.where(is_upper, partner, current)
        scaled = jnp.stack(
            [factor[0] * w_real - factor[1] * w_imag, factor[0] * w_imag + factor[1] * w_real]
        )
        current = jnp.where(is_upper, base_val - scaled, base_val + scaled)
    conv_out = (
        current[0, 0] + current[0, 1] * jnp.cos(start_phase) - current[1, 1] * jnp.sin(start_phase)
    ) / full_len
    mixed_out = (query_part * (conv_out + med_out + skip_gain * signal)).astype(jnp.bfloat16)
    return jnp.dot(mixed_out, w_out, preferred_element_type=jnp.float32).astype(jnp.bfloat16)


def solution(mesh):
    placed = (P(("groups", "seq"), None), P(), P(), P(), P("seq", None), P(), P(), P())
    return jax.shard_map(
        local, mesh=mesh, in_specs=placed, out_specs=P(("groups", "seq"), None), check_vma=False
    )
```

profile of v0, /device:TPU:0, one launch (start us, length us, event | category | flops | bytes accessed | tf_op | source)
XLA Modules:
  0.0 211.3 jit_solution(2216791617882985086)
XLA Ops:
  0.0 1.1 fusion.23
  1.1 1.2 convolution_convert_fusion
  2.4 2.4 %collective-permute-start = (bf16[2,768]{1,0:T(2,128)(2,1)S(1)}, bf16[2,768]{1,0:T(2,128)(2,1)S(1)}, u32[]{:S(2)}, u32[]{:S(2)}) collective-permute-start(bf16[2,768]{1,0:T(2,128)(2,1)S(1)} %slice.163), channel_id=1, source_target_pairs={{0,1},{1,2},{2,3},{3,4},{4,5},{5,6},{6,7},{7,8},{8,9},{9,10},{10,1... | collective-permute-start | bytes 9224 | tf_op jit(solution)/shard_map/ppermute | solution.py:15
  7.1 1.3 fusion.13
  8.3 6.5 %collective-permute-start.1 = (bf16[2,2,2,256,256]{4,3,2,1,0:T(8,128)(2,1)}, bf16[2,2,2,256,256]{4,3,2,1,0:T(8,128)(2,1)S(1)}, u32[]{:S(2)}, u32[]{:S(2)}) collective-permute-start(bf16[2,2,2,256,256]{4,3,2,1,0:T(8,128)(2,1)} %fusion.13), channel_id=1, source_target_pairs={{0,8},{1,9},{2,10},{3,11},{4,12},{5,13},{6,14},{7,15},{8,0},{9,1},... | collective-permute-start | bytes 3145736 | tf_op jit(solution)/shard_map/ppermute | solution.py:19
  15.0 44.6 %collective-permute-done.1 = bf16[2,2,2,256,256]{4,3,2,1,0:T(8,128)(2,1)S(1)} collective-permute-done((bf16[2,2,2,256,256]{4,3,2,1,0:T(8,128)(2,1)}, bf16[2,2,2,256,256]{4,3,2,1,0:T(8,128)(2,1)S(1)}, u32[]{:S(2)}, u32[]{:S(2)}) %collective-permute-start.1) | collective-permute-done | bytes 1048608 | tf_op jit(solution)/shard_map/ppermute | solution.py:19
  60.6 2.9 %fusion.109 = (bf16[2,2,2,256,256]{4,3,2,1,0:T(8,128)(2,1)}, f32[2,2,2,256,256]{4,3,2,1,0:T(8,128)S(1)}) fusion(bf16[2,2,2,256,256]{4,3,2,1,0:T(8,128)(2,1)} %copy-done.6, f32[1,2,2,256,256]{4,3,2,1,0:T(8,128)} %copy-done.3, f32[1,2,2,256,256]{4,3,2,1,0:T(8,128)S(1)} %get-tuple-element.227, f32[1,2,2,256,256]{4,3,2,1,0:T(8,128)S(1)} %get-tuple-element.212, ...), kind=kLoop, calls=%fused_computation.189 | loop fusion | flops 3145728 | bytes 8388609 | tf_op jit(solution)/shard_map/convert_element_type | solution.py:105
  64.5 23.4 %collective-permute-done.2 = bf16[2,2,2,256,256]{4,3,2,1,0:T(8,128)(2,1)S(1)} collective-permute-done((bf16[2,2,2,256,256]{4,3,2,1,0:T(8,128)(2,1)}, bf16[2,2,2,256,256]{4,3,2,1,0:T(8,128)(2,1)S(1)}, u32[]{:S(2)}, u32[]{:S(2)}) %collective-permute-start.2) | collective-permute-done | bytes 1048608 | tf_op jit(solution)/shard_map/ppermute | solution.py:19
  89.1 3.2 %fusion.107 = (bf16[2,2,2,256,256]{4,3,2,1,0:T(8,128)(2,1)}, f32[2,2,2,256,256]{4,3,2,1,0:T(8,128)S(1)}) fusion(f32[2,2,2,256,256]{4,3,2,1,0:T(8,128)} %copy-done.1, bf16[2,2,2,256,256]{4,3,2,1,0:T(8,128)(2,1)} %copy-done.7, f32[1,2,2,256,256]{4,3,2,1,0:T(8,128)S(1)} %get-tuple-element.210, f32[1,2,2,256,256]{4,3,2,1,0:T(8,128)S(1)} %get-tuple-element.209, ...), kind=kLoop, calls=%fused_computation.188 | loop fusion | flops 2621440 | bytes 8388609 | tf_op jit(solution)/shard_map/convert_element_type | solution.py:105
  92.3 1.4 collective-permute-start.3
  94.0 22.2 %collective-permute-done.3 = bf16[2,2,2,256,256]{4,3,2,1,0:T(8,128)(2,1)S(1)} collective-permute-done((bf16[2,2,2,256,256]{4,3,2,1,0:T(8,128)(2,1)}, bf16[2,2,2,256,256]{4,3,2,1,0:T(8,128)(2,1)S(1)}, u32[]{:S(2)}, u32[]{:S(2)}) %collective-permute-start.3) | collective-permute-done | bytes 1048608 | tf_op jit(solution)/shard_map/ppermute | solution.py:19
  116.6 2.1 fusion.105
  119.0 2.5 %collective-permute-done.4 = bf16[2,2,2,256,256]{4,3,2,1,0:T(8,128)(2,1)S(1)} collective-permute-done((bf16[2,2,2,256,256]{4,3,2,1,0:T(8,128)(2,1)}, bf16[2,2,2,256,256]{4,3,2,1,0:T(8,128)(2,1)S(1)}, u32[]{:S(2)}, u32[]{:S(2)}) %collective-permute-start.4) | collective-permute-done | bytes 1048608 | tf_op jit(solution)/shard_map/ppermute | solution.py:19
  121.6 1.8 convert_subtract_fusion
  123.7 1.3 copy-done.2
  125.5 2.8 %fusion.45 = f32[2,2,256,256]{3,2,1,0:T(8,128)S(1)} fusion(f32[2,2,2,256,256]{4,3,2,1,0:T(8,128)S(1)} %fusion.10, f32[2,256]{1,0:T(2,128)S(1)} %get-tuple-element.226, f32[2,256]{1,0:T(2,128)S(1)} %get-tuple-element.225), kind=kOutput, calls=%fused_computation.128 | convolution fusion | flops 807010304 | bytes 3149824 | tf_op jit(solution)/shard_map/kt,setd->sekd/dot_general | solution.py:44
  128.3 2.8 %fusion.43 = f32[2,2,256,256]{3,2,1,0:T(8,128)S(1)} fusion(f32[2,2,2,256,256]{4,3,2,1,0:T(8,128)S(1)} %fusion.10, f32[2,256]{1,0:T(2,128)S(1)} %get-tuple-element.226, f32[2,256]{1,0:T(2,128)S(1)} %get-tuple-element.225), kind=kOutput, calls=%fused_computation.126 | convolution fusion | flops 807010304 | bytes 3149824 | tf_op jit(solution)/shard_map/kt,setd->sekd/dot_general | solution.py:47
  131.1 3.0 %fusion.12 = f32[2,2,256,256]{2,3,1,0:T(8,128)S(1)} fusion(f32[2,2,256,256]{3,2,1,0:T(8,128)S(1)} %fusion.45, f32[2,2,2,256,256]{4,3,2,1,0:T(8,128)S(1)} %fusion.10, f32[2,256]{1,0:T(2,128)S(1)} %get-tuple-element.226, f32[2,256]{1,0:T(2,128)S(1)} %get-tuple-element.225), kind=kOutput, calls=%fused_computation.32 | convolution fusion | flops 807272448 | bytes 4198400 | tf_op jit(solution)/shard_map/kt,setd->sekd/dot_general | solution.py:44
  134.1 2.8 %fusion.11 = f32[2,2,256,256]{2,3,1,0:T(8,128)S(1)} fusion(f32[2,2,256,256]{3,2,1,0:T(8,128)S(1)} %fusion.43, f32[2,2,2,256,256]{4,3,2,1,0:T(8,128)S(1)} %fusion.10, f32[2,256]{1,0:T(2,128)S(1)} %get-tuple-element.226, f32[2,256]{1,0:T(2,128)S(1)} %get-tuple-element.225), kind=kOutput, calls=%fused_computation.30 | convolution fusion | flops 807272448 | bytes 4198400 | tf_op jit(solution)/shard_map/kt,setd->sekd/dot_general | solution.py:47
  137.0 1.6 fusion.15
  138.6 1.6 fusion.19
  140.2 1.6 convolution_add_fusion.1
  141.8 1.7 subtract_bitcast_fusion
  144.0 1.6 collective-permute-done.5
  145.9 1.0 fusion.104
  148.0 13.1 %collective-permute-done.6 = bf16[2,2,256,256]{3,2,1,0:T(8,128)(2,1)S(1)} collective-permute-done((bf16[2,2,256,256]{3,2,1,0:T(8,128)(2,1)}, bf16[2,2,256,256]{3,2,1,0:T(8,128)(2,1)S(1)}, u32[]{:S(2)}, u32[]{:S(2)}) %collective-permute-start.6) | collective-permute-done | bytes 524320 | tf_op jit(solution)/shard_map/ppermute | solution.py:19
  161.3 1.0 fusion.103
  162.3 2.4 %collective-permute-start.7 = (bf16[2,2,256,256]{3,2,1,0:T(8,128)(2,1)}, bf16[2,2,256,256]{3,2,1,0:T(8,128)(2,1)S(1)}, u32[]{:S(2)}, u32[]{:S(2)}) collective-permute-start(bf16[2,2,256,256]{3,2,1,0:T(8,128)(2,1)} %get-tuple-element.185), channel_id=1, source_target_pairs={{0,4},{1,5},{2,6},{3,7},{4,0},{5,1},{6,2},{7,3},{8,12},{9,13},{10,... | collective-permute-start | bytes 1572872 | tf_op jit(solution)/shard_map/ppermute | solution.py:19
  164.8 1.3 collective-permute-start.9
  167.0 9.3 %collective-permute-done.7 = bf16[2,2,256,256]{3,2,1,0:T(8,128)(2,1)S(1)} collective-permute-done((bf16[2,2,256,256]{3,2,1,0:T(8,128)(2,1)}, bf16[2,2,256,256]{3,2,1,0:T(8,128)(2,1)S(1)}, u32[]{:S(2)}, u32[]{:S(2)}) %collective-permute-start.7) | collective-permute-done | bytes 524320 | tf_op jit(solution)/shard_map/ppermute | solution.py:19
  177.1 2.1 fusion.102
  179.2 3.6 %collective-permute-start.8 = (bf16[2,2,256,256]{3,2,1,0:T(8,128)(2,1)}, bf16[2,2,256,256]{3,2,1,0:T(8,128)(2,1)S(1)}, u32[]{:S(2)}, u32[]{:S(2)}) collective-permute-start(bf16[2,2,256,256]{3,2,1,0:T(8,128)(2,1)} %get-tuple-element.183), channel_id=1, source_target_pairs={{0,8},{1,9},{2,10},{3,11},{4,12},{5,13},{6,14},{7,15},{8,0},{9,1},... | collective-permute-start | bytes 1572872 | tf_op jit(solution)/shard_map/ppermute | solution.py:19
  182.8 23.6 %while.17 = (s32[]{:T(128)}, f32[256,256]{1,0:T(8,128)S(1)}, f32[128,256]{1,0:T(8,128)}, f32[383,256]{1,0:T(8,128)S(1)}, s32[]{:T(128)}, /*index=5*/s32[]{:T(128...) while((s32[]{:T(128)}, f32[256,256]{1,0:T(8,128)S(1)}, ...), condition=%wide.region_2.0_spmd.clone, body=%wide.region_1.0_spmd.clone.sunk | while | flops 1114179 | bytes 2647031 | solution.py:95
  184.2 1.0 constant_dynamic-slice_fusion.9
  185.7 1.0 constant_dynamic-slice_fusion.9
  187.2 1.0 constant_dynamic-slice_fusion.9
  188.7 1.0 constant_dynamic-slice_fusion.9
  190.2 1.0 constant_dynamic-slice_fusion.9
  191.6 1.0 constant_dynamic-slice_fusion.9
  193.1 1.0 constant_dynamic-slice_fusion.9
  194.6 1.0 constant_dynamic-slice_fusion.9
  196.1 1.0 constant_dynamic-slice_fusion.9
  197.5 1.0 constant_dynamic-slice_fusion.9
  199.0 1.0 constant_dynamic-slice_fusion.9
  200.5 1.0 constant_dynamic-slice_fusion.9
  202.0 1.0 constant_dynamic-slice_fusion.9
  207.2 1.2 convert_select_fusion
  209.4 1.8 convolution_convert_fusion.1
  (87 shorter events, 19.5 us)
Async XLA Ops:
  0.0 1.1 copy-start
  0.0 6.1 %copy-start.11 = (f32[256,256]{1,0:T(8,128)S(1)}, f32[256,256]{1,0:T(8,128)}, u32[]{:S(2)}) copy-start(f32[256,256]{1,0:T(8,128)} %param.14) | copy-start | bytes 786436
  2.4 3.4 %collective-permute-start = (bf16[2,768]{1,0:T(2,128)(2,1)S(1)}, bf16[2,768]{1,0:T(2,128)(2,1)S(1)}, u32[]{:S(2)}, u32[]{:S(2)}) collective-permute-start(bf16[2,768]{1,0:T(2,128)(2,1)S(1)} %slice.163), channel_id=1, source_target_pairs={{0,1},{1,2},{2,3},{3,4},{4,5},{5,6},{6,7},{7,8},{8,9},{9,10},{10,1... | collective-permute-start | bytes 9224 | tf_op jit(solution)/shard_map/ppermute | solution.py:15
  6.0 0.9 copy-start.4
  7.1 52.8 %copy-start.3 = (f32[1,2,2,256,256]{4,3,2,1,0:T(8,128)}, f32[1,2,2,256,256]{4,3,2,1,0:T(8,128)S(1)}, u32[]{:S(2)}) copy-start(f32[1,2,2,256,256]{4,3,2,1,0:T(8,128)S(1)} %get-tuple-element.228) | copy-start | bytes 3145732
  8.3 51.3 %collective-permute-start.1 = (bf16[2,2,2,256,256]{4,3,2,1,0:T(8,128)(2,1)}, bf16[2,2,2,256,256]{4,3,2,1,0:T(8,128)(2,1)S(1)}, u32[]{:S(2)}, u32[]{:S(2)}) collective-permute-start(bf16[2,2,2,256,256]{4,3,2,1,0:T(8,128)(2,1)} %fusion.13), channel_id=1, source_target_pairs={{0,8},{1,9},{2,10},{3,11},{4,12},{5,13},{6,14},{7,15},{8,0},{9,1},... | collective-permute-start | bytes 3145736 | tf_op jit(solution)/shard_map/ppermute | solution.py:19
  59.6 1.0 copy-start.6
  63.5 24.6 %copy-start.1 = (f32[2,2,2,256,256]{4,3,2,1,0:T(8,128)}, f32[2,2,2,256,256]{4,3,2,1,0:T(8,128)S(1)}, u32[]{:S(2)}) copy-start(f32[2,2,2,256,256]{4,3,2,1,0:T(8,128)S(1)} %get-tuple-element.194) | copy-start | bytes 6291460
  63.6 24.3 %collective-permute-start.2 = (bf16[2,2,2,256,256]{4,3,2,1,0:T(8,128)(2,1)}, bf16[2,2,2,256,256]{4,3,2,1,0:T(8,128)(2,1)S(1)}, u32[]{:S(2)}, u32[]{:S(2)}) collective-permute-start(bf16[2,2,2,256,256]{4,3,2,1,0:T(8,128)(2,1)} %get-tuple-element.193), channel_id=1, source_target_pairs={{0,4},{1,5},{2,6},{3,7},{4,0},{5,1},{6,2},{7,3},{8,12},{9,13},{10,... | collective-permute-start | bytes 3145736 | tf_op jit(solution)/shard_map/ppermute | solution.py:19
  87.9 1.0 copy-start.7
  92.3 23.8 %collective-permute-start.3 = (bf16[2,2,2,256,256]{4,3,2,1,0:T(8,128)(2,1)}, bf16[2,2,2,256,256]{4,3,2,1,0:T(8,128)(2,1)S(1)}, u32[]{:S(2)}, u32[]{:S(2)}) collective-permute-start(bf16[2,2,2,256,256]{4,3,2,1,0:T(8,128)(2,1)} %get-tuple-element.191), channel_id=1, source_target_pairs={{0,2},{1,3},{2,0},{3,1},{4,6},{5,7},{6,4},{7,5},{8,10},{9,11},{10,... | collective-permute-start | bytes 3145736 | tf_op jit(solution)/shard_map/ppermute | solution.py:19
  118.7 2.9 %collective-permute-start.4 = (bf16[2,2,2,256,256]{4,3,2,1,0:T(8,128)(2,1)}, bf16[2,2,2,256,256]{4,3,2,1,0:T(8,128)(2,1)S(1)}, u32[]{:S(2)}, u32[]{:S(2)}) collective-permute-start(bf16[2,2,2,256,256]{4,3,2,1,0:T(8,128)(2,1)} %get-tuple-element.189), channel_id=1, source_target_pairs={{0,1},{1,0},{2,3},{3,2},{4,5},{5,4},{6,7},{7,6},{8,9},{9,8},{10,11... | collective-permute-start | bytes 3145736 | tf_op jit(solution)/shard_map/ppermute | solution.py:19
  123.5 1.6 copy-start.2
  143.6 2.0 collective-permute-start.5
  146.9 14.2 %collective-permute-start.6 = (bf16[2,2,256,256]{3,2,1,0:T(8,128)(2,1)}, bf16[2,2,256,256]{3,2,1,0:T(8,128)(2,1)S(1)}, u32[]{:S(2)}, u32[]{:S(2)}) collective-permute-start(bf16[2,2,256,256]{3,2,1,0:T(8,128)(2,1)} %get-tuple-element.187), channel_id=1, source_target_pairs={{0,2},{1,3},{2,0},{3,1},{4,6},{5,7},{6,4},{7,5},{8,10},{9,11},{10,... | collective-permute-start | bytes 1572872 | tf_op jit(solution)/shard_map/ppermute | solution.py:19
  161.3 3.4 %copy-start.5 = (f32[256,768]{1,0:T(8,128)S(1)}, f32[256,768]{1,0:T(8,128)}, u32[]{:S(2)}) copy-start(f32[256,768]{1,0:T(8,128)} %copy-done.4) | copy-start | bytes 2359300
  162.3 14.0 %collective-permute-start.7 = (bf16[2,2,256,256]{3,2,1,0:T(8,128)(2,1)}, bf16[2,2,256,256]{3,2,1,0:T(8,128)(2,1)S(1)}, u32[]{:S(2)}, u32[]{:S(2)}) collective-permute-start(bf16[2,2,256,256]{3,2,1,0:T(8,128)(2,1)} %get-tuple-element.185), channel_id=1, source_target_pairs={{0,4},{1,5},{2,6},{3,7},{4,0},{5,1},{6,2},{7,3},{8,12},{9,13},{10,... | collective-permute-start | bytes 1572872 | tf_op jit(solution)/shard_map/ppermute | solution.py:19
  164.8 2.2 %collective-permute-start.9 = (bf16[127,256]{1,0:T(8,128)(2,1)S(1)}, bf16[127,256]{1,0:T(8,128)(2,1)S(1)}, u32[]{:S(2)}, u32[]{:S(2)}) collective-permute-start(bf16[127,256]{1,0:T(8,128)(2,1)S(1)} %slice.293), channel_id=1, source_target_pairs={{0,1},{1,2},{2,3},{3,4},{4,5},{5,6},{6,7},{7,8},{8,9},{9,10},{10,1... | collective-permute-start | bytes 195080 | tf_op jit(solution)/shard_map/ppermute | solution.py:15
  176.3 0.8 copy-start.8
  179.2 27.2 %collective-permute-start.8 = (bf16[2,2,256,256]{3,2,1,0:T(8,128)(2,1)}, bf16[2,2,256,256]{3,2,1,0:T(8,128)(2,1)S(1)}, u32[]{:S(2)}, u32[]{:S(2)}) collective-permute-start(bf16[2,2,256,256]{3,2,1,0:T(8,128)(2,1)} %get-tuple-element.183), channel_id=1, source_target_pairs={{0,8},{1,9},{2,10},{3,11},{4,12},{5,13},{6,14},{7,15},{8,0},{9,1},... | collective-permute-start | bytes 1572872 | tf_op jit(solution)/shard_map/ppermute | solution.py:19
  206.4 0.8 copy-start.9
  207.2 1.4 copy-start.10
  208.5 0.9 copy-start.12
  208.5 0.9 copy-start.13
where the time goes:
time: 213 us; the launch traced here: 211 us
  waiting for transfers between devices  117 us (55%)
  other arithmetic  26.9 us (13%)
  local copies, waits for them, and re-layouts  22.4 us (11%)
  matrix products  21 us (10%)
  starting transfers between devices  19.4 us (9%)
  loops' own time  2.25 us (1%)
    ppermute x8, waiting for transfers between devices, from_partner(): lax.ppermute(array, axis, [(i, i ^ 1 << distance) for i in range(lax.axis...  117 us
    dynamic_slice x16, local copies, waits for them, and re-layouts, add_group(): weights = lax.dynamic_slice_in_dim(medium_filter, tap_num, 1, 0)  16.2 us
    ppermute x8, starting transfers between devices, from_partner(): lax.ppermute(array, axis, [(i, i ^ 1 << distance) for i in range(lax.axis...  15.8 us
    convert_element_type x8, other arithmetic, local(): current.astype(jnp.bfloat16)  13.7 us
    unnamed x28, local copies, waits for them, and re-layouts  5.32 us
    add x16, other arithmetic, add_group(): acc = acc + weights * window  5.1 us
  transfers between devices with their start and end apart: 10, of which 8 were waited for; matrix products, arithmetic and copies ran while one was open for 11% of the time, Pallas kernels for 0%

commit v1 on v0

v1 whole, which is shorter than its diff:
```python
import math

import jax
import jax.numpy as jnp
import numpy as np
from jax import lax
from jax.experimental import pallas as pl
from jax.experimental.pallas import tpu as pltpu
from jax.sharding import PartitionSpec as P

epsilon = 1e-06
rim_pad = 16
vmem_bytes = 32 * 2**20


def from_behind(array, axis, by):
    devices = lax.axis_size(axis)
    pairs = [(i, i + by) for i in range(devices) if 0 <= i + by < devices]
    return lax.ppermute(array, axis, pairs)


def call(body, outs, args, scratch=(), flops=0, moved=0):
    return pl.pallas_call(
        body,
        out_shape=outs,
        in_specs=[pl.BlockSpec(memory_space=pltpu.VMEM)] * len(args),
        out_specs=jax.tree.map(lambda _: pl.BlockSpec(memory_space=pltpu.VMEM), outs),
        scratch_shapes=list(scratch),
        compiler_params=pltpu.CompilerParams(vmem_limit_bytes=vmem_bytes),
        cost_estimate=pl.CostEstimate(flops=flops, bytes_accessed=moved, transcendentals=0),
    )(*args)


def spectral_tables(devices, rows, chans):
    span = 2 * devices
    full_len = span * rows
    freq_count = devices + 1
    height = -(-freq_count * chans // 16) * 16
    freqs = np.arange(freq_count)
    blocks = np.arange(devices)
    offsets = np.arange(rows)
    eye = np.eye(chans)

    def grown(table):
        out = np.zeros((height, table.shape[1]))
        out[: table.shape[0]] = table
        return out

    angle = 2.0 * math.pi / span * (freqs[:, None] * blocks[None, :] % span)
    first = np.concatenate([grown(np.kron(np.cos(angle), eye)), grown(np.kron(-np.sin(angle), eye))])
    weight = np.where((freqs == 0) | (freqs == devices), 1.0, 2.0)[:, None] / full_len
    last = np.concatenate(
        [grown(np.kron(weight * np.cos(angle), eye)), grown(np.kron(-weight * np.sin(angle), eye))]
    ).T
    twist = 2.0 * math.pi / full_len * (freqs[:, None] * offsets[None, :] % full_len)
    tw_cos = grown(np.repeat(np.cos(twist), chans, axis=0))
    tw_sin = grown(np.repeat(np.sin(twist), chans, axis=0))
    turn = 2.0 * math.pi / rows * (offsets[:, None] * offsets[None, :] % rows)
    inner = np.concatenate([np.cos(turn), np.sin(turn)], axis=1)
    return (
        jnp.asarray(first, jnp.bfloat16),
        jnp.asarray(np.concatenate([tw_cos, tw_sin]), jnp.float32),
        jnp.asarray(inner, jnp.bfloat16),
        jnp.asarray(last, jnp.bfloat16),
    )


def filter_body(long_ref, medium_ref, skip_ref, out_ref):
    med_len = medium_ref.shape[0]
    is_first = jnp.where(lax.axis_index("seq") == 0, 1.0, 0.0)
    head = long_ref[0:med_len, :] + is_first * medium_ref[...]
    row = lax.broadcasted_iota(jnp.int32, head.shape, 0)
    head = head + jnp.where(row == 0, is_first * skip_ref[...], 0.0)
    out_ref[:, 0:med_len] = head.T.astype(jnp.bfloat16)
    out_ref[:, med_len:] = long_ref[med_len:, :].T.astype(jnp.bfloat16)


def signal_body(tokens_ref, rim_ref, gain_ref, w_ref, short_ref, signal_ref, query_ref, proj_ref):
    rows, width = tokens_ref.shape
    for src, begin, count in ((rim_ref, 0, rim_pad), (tokens_ref, rim_pad, rows)):
        inputs = src[...].astype(jnp.float32)
        mean_sq = jnp.mean(inputs * inputs, axis=-1, keepdims=True)
        normed = (inputs * lax.rsqrt(mean_sq + epsilon) * gain_ref[...]).astype(jnp.bfloat16)
        projected = jnp.dot(normed, w_ref[...], preferred_element_type=jnp.float32)
        proj_ref[begin : begin + count, :] = projected.astype(jnp.bfloat16).astype(jnp.float32)
    taps_count = short_ref.shape[0]

    def mixed(part):
        cols = slice(part * width, (part + 1) * width)
        acc = short_ref[0:1, cols] * proj_ref[rim_pad : rim_pad + rows, cols]
        for tap_num in range(1, taps_count):
            begin = rim_pad - tap_num
            acc = acc + short_ref[tap_num : tap_num + 1, cols] * proj_ref[begin : begin + rows, cols]
        return acc

    query_ref[...] = mixed(0)
    signal_ref[...] = (mixed(1) * mixed(2)).T.astype(jnp.bfloat16)


def forward(values, first_ref, twist_ref, inner_ref):
    half = twist_ref.shape[0] // 2
    rows = twist_ref.shape[1]
    spread = jnp.dot(first_ref[...], values, preferred_element_type=jnp.float32)
    tw_cos, tw_sin = twist_ref[0:half, :], twist_ref[half:, :]
    real, imag = spread[0:half], spread[half:]
    turned = jnp.concatenate([real * tw_cos + imag * tw_sin, imag * tw_cos - real * tw_sin])
    both = jnp.dot(turned.astype(jnp.bfloat16), inner_ref[...], preferred_element_type=jnp.float32)
    return both[0:half, 0:rows] + both[half:, rows:], both[half:, 0:rows] - both[0:half, rows:]


def filter_spectrum_body(filter_ref, first_ref, twist_ref, inner_ref, out_ref):
    half = twist_ref.shape[0] // 2
    real, imag = forward(filter_ref[...], first_ref, twist_ref, inner_ref)
    out_ref[0:half, :] = real
    out_ref[half:, :] = imag


def convolve_body(signal_ref, spec_ref, first_ref, twist_ref, inner_ref, last_ref, out_ref):
    half = twist_ref.shape[0] // 2
    rows = twist_ref.shape[1]
    real, imag = forward(signal_ref[...], first_ref, twist_ref, inner_ref)
    fil_re, fil_im = spec_ref[0:half, :], spec_ref[half:, :]
    product = jnp.concatenate([real * fil_re - imag * fil_im, real * fil_im + imag * fil_re])
    both = jnp.dot(product.astype(jnp.bfloat16), inner_ref[...], preferred_element_type=jnp.float32)
    real = both[0:half, 0:rows] - both[half:, rows:]
    imag = both[half:, 0:rows] + both[0:half, rows:]
    tw_cos, tw_sin = twist_ref[0:half, :], twist_ref[half:, :]
    turned = jnp.concatenate([real * tw_cos - imag * tw_sin, imag * tw_cos + real * tw_sin])
    out_ref[...] = jnp.dot(
        last_ref[...], turned.astype(jnp.bfloat16), preferred_element_type=jnp.float32
    ).astype(jnp.bfloat16)


def output_body(conv_ref, query_ref, w_ref, out_ref):
    conv = conv_ref[...].astype(jnp.float32).T
    mixed_out = (query_ref[...] * conv).astype(jnp.bfloat16)
    out_ref[...] = jnp.dot(mixed_out, w_ref[...], preferred_element_type=jnp.float32).astype(
        jnp.bfloat16
    )


def local(tokens, norm_gain, w_in, short_filter, long_filter, medium_filter, skip_gain, w_out):
    rows, width = tokens.shape
    devices = lax.axis_size("seq")
    chans = width // devices
    first, twist, inner, last = spectral_tables(devices, rows, chans)
    flat = jax.ShapeDtypeStruct((width, rows), jnp.bfloat16)

    def swap(array):
        return lax.all_to_all(
            array.reshape(devices, chans, rows), "seq", split_axis=0, concat_axis=0
        ).reshape(width, rows)

    rim = from_behind(tokens[rows - rim_pad :], "seq", 1)
    filter_part = call(
        filter_body, flat, (long_filter, medium_filter, skip_gain[None, :]), moved=500_000
    )
    filter_part = swap(filter_part)
    signal, query = call(
        signal_body,
        (flat, jax.ShapeDtypeStruct((rows, width), jnp.float32)),
        (tokens, rim, norm_gain[None, :], w_in, short_filter),
        [pltpu.VMEM((rim_pad + rows, 3 * width), jnp.float32)],
        flops=2 * rows * width * 3 * width,
        moved=1_000_000,
    )
    signal = swap(signal)
    work = 2 * first.shape[0] * width * rows
    spectrum = call(
        filter_spectrum_body,
        jax.ShapeDtypeStruct(twist.shape, jnp.float32),
        (filter_part, first, twist, inner),
        flops=3 * work,
        moved=1_500_000,
    )
    conv = call(
        convolve_body,
        flat,
        (signal, spectrum, first, twist, inner, last),
        flops=6 * work,
        moved=2_000_000,
    )
    conv = swap(conv)
    return call(
        output_body,
        jax.ShapeDtypeStruct((rows, width), jnp.bfloat16),
        (conv, query, w_out),
        flops=2 * rows * width * width,
        moved=600_000,
    )


def solution(mesh):
    placed = (P(("groups", "seq"), None), P(), P(), P(), P("seq", None), P(), P(), P())
    return jax.shard_map(
        local, mesh=mesh, in_specs=placed, out_specs=P(("groups", "seq"), None), check_vma=False
    )
```

time: 213 us -> 47.4 us (0.22)
  waiting for transfers between devices: 117 us -> 8.65 us
  other arithmetic: 26.9 us -> 0 us
  matrix products: 21 us -> 0 us
  local copies, waits for them, and re-layouts: 22.4 us -> 5.55 us
  blocking collectives: 0 us -> 10.7 us
  Pallas kernels: 0 us -> 4.78 us
  starting transfers between devices: 19.4 us -> 17.1 us
  loops' own time: 2.25 us -> 0 us
    ppermute x8 -> x0, waiting for transfers between devices: 117 us -> none  [from_partner(): lax.ppermute(array, axis, [(i, i ^ 1 << distance) for i in range(lax.axis...]
    dot_general x10 -> x0, matrix products: 21 us -> none  [the longest x1 2.98 us: spectral_middle(): jnp.einsum('kt,setd->sekd', sin_table, imag_part, precision=highest)]
    dynamic_slice x16 -> x0, local copies, waits for them, and re-layouts: 16.2 us -> none  [add_group(): weights = lax.dynamic_slice_in_dim(medium_filter, tap_num, 1, 0)]
    ppermute x8 -> x0, starting transfers between devices: 15.8 us -> none  [from_partner(): lax.ppermute(array, axis, [(i, i ^ 1 << distance) for i in range(lax.axis...]
    all_to_all x0 -> x2, starting transfers between devices: none -> 14.8 us  [swap(): lax.all_to_all(array.reshape(devices, chans, rows), 'seq', split_axis=0,...]
    convert_element_type x9 -> x0, other arithmetic: 13.7 us -> none  [the longest x8 13.7 us: local(): current.astype(jnp.bfloat16)]
    all_to_all x0 -> x1, blocking collectives: none -> 10.7 us  [swap(): lax.all_to_all(array.reshape(devices, chans, rows), 'seq', split_axis=0,...]
    all_to_all x0 -> x2, waiting for transfers between devices: none -> 7.84 us  [swap(): lax.all_to_all(array.reshape(devices, chans, rows), 'seq', split_axis=0,...]
  transfers between devices with their start and end apart: 10 -> 3, of which waited for: 8 -> 3; matrix products, arithmetic and copies ran while one was open for 11% -> 1% of each run, Pallas kernels for 0% -> 4%
where the time goes in v1:
time: 47.4 us; the launch traced here: 46.9 us
  starting transfers between devices  17.1 us (36%)
  blocking collectives  10.7 us (23%)
  waiting for transfers between devices  8.65 us (18%)
  local copies, waits for them, and re-layouts  5.55 us (12%)
  Pallas kernels  4.78 us (10%)
    all_to_all x2, starting transfers between devices, swap(): lax.all_to_all(array.reshape(devices, chans, rows), 'seq', split_axis=0,...  14.8 us
    all_to_all x1, blocking collectives, swap(): lax.all_to_all(array.reshape(devices, chans, rows), 'seq', split_axis=0,...  10.7 us
    all_to_all x2, waiting for transfers between devices, swap(): lax.all_to_all(array.reshape(devices, chans, rows), 'seq', split_axis=0,...  7.84 us
    unnamed x24, local copies, waits for them, and re-layouts  4.85 us
    pallas_call x5, Pallas kernels, call(): pl.pallas_call(body, out_shape=outs, in_specs=[pl.BlockSpec(memory_space=...  4.78 us
    ppermute x1, starting transfers between devices, from_behind(): return lax.ppermute(array, axis, pairs)  2.3 us
  transfers between devices with their start and end apart: 3, of which 3 were waited for; matrix products, arithmetic and copies ran while one was open for 1% of the time, Pallas kernels for 4%

profile of v1, /device:TPU:0, one launch (start us, length us, event | category | flops | bytes accessed | tf_op | source)
XLA Modules:
  0.0 46.9 jit_solution(1558397585462243853)
XLA Ops:
  0.0 0.0 copy-start.10
  0.0 0.7 %copy-done.10 = f32[256]{0:T(256)S(1)} copy-done((f32[256]{0:T(256)S(1)}, f32[256]{0:T(256)}, u32[]{:S(2)}) %copy-start.10) | copy-done | bytes 1048
  0.7 0.0 copy-start.5
  0.7 0.9 %copy-done.5 = f32[256,256]{1,0:T(8,128)S(1)} copy-done((f32[256,256]{1,0:T(8,128)S(1)}, f32[256,256]{1,0:T(8,128)}, u32[]{:S(2)}) %copy-start.5) | copy-done | bytes 262168
  1.6 0.0 copy-start.8
  1.6 0.9 %copy-done.8 = f32[128,256]{1,0:T(8,128)S(1)} copy-done((f32[128,256]{1,0:T(8,128)S(1)}, f32[128,256]{1,0:T(8,128)}, u32[]{:S(2)}) %copy-start.8) | copy-done | bytes 131096
  2.5 0.0 copy-start.3
  2.5 0.0 copy-start.2
  2.5 0.8 %shard_map.119 = bf16[256,256]{1,0:T(8,128)(2,1)} custom-call(f32[256,256]{1,0:T(8,128)S(1)} %copy-done.5, f32[128,256]{1,0:T(8,128)S(1)} %copy-done.8, f32[1,256]{1,0:T(1,128)S(1)} %bitcast.12), custom_call_target="tpu_custom_call" | custom-call | bytes 500000 | tf_op jit(solution)/shard_map/pallas_call | solution.py:23
  3.3 0.0 copy-start
  3.3 7.5 %all-to-all-start.1 = ((bf16[16,16,256]{2,1,0:T(8,128)(2,1)}), bf16[16,16,256]{2,1,0:T(8,128)(2,1)S(1)}, u32[]{:S(2)}, u32[]{:S(2)}) async-start(bf16[16,16,256]{2,1,0:T(8,128)(2,1)} %bitcast.4), calls=%async_computation.1 | async-start | bytes 262144 | tf_op jit(solution)/shard_map/all_to_all | solution.py:150
  10.8 0.7 %slice.3 = bf16[16,256]{1,0:T(8,128)(2,1)S(1)} slice(bf16[256,256]{1,0:T(8,128)(2,1)} %tokens_ref.1), slice={[240:256], [0:256]} | slice | bytes 16384 | tf_op jit(solution)/shard_map/slice | solution.py:154
  11.5 2.3 %collective-permute-start = (bf16[16,256]{1,0:T(8,128)(2,1)S(1)}, bf16[16,256]{1,0:T(8,128)(2,1)S(1)}, u32[]{:S(2)}, u32[]{:S(2)}) collective-permute-start(bf16[16,256]{1,0:T(8,128)(2,1)S(1)} %slice.3), channel_id=1, source_target_pairs={{0,1},{1,2},{2,3},{3,4},{4,5},{5,6},{6,7},{7,8},{8,9},{9,10},{10,1... | collective-permute-start | bytes 24584 | tf_op jit(solution)/shard_map/ppermute | solution.py:19
  13.8 0.8 %collective-permute-done.rim_ref = bf16[16,256]{1,0:T(8,128)(2,1)S(1)} collective-permute-done((bf16[16,256]{1,0:T(8,128)(2,1)S(1)}, bf16[16,256]{1,0:T(8,128)(2,1)S(1)}, u32[]{:S(2)}, u32[]{:S(2)}) %collective-permute-start) | collective-permute-done | bytes 8224 | tf_op jit(solution)/shard_map/ppermute | solution.py:19
  14.7 0.0 copy-done.3
  14.7 0.0 copy-start.6
  14.7 0.9 %copy-done.6 = bf16[256,256]{1,0:T(8,128)(2,1)S(1)} copy-done((bf16[256,256]{1,0:T(8,128)(2,1)S(1)}, bf16[256,256]{1,0:T(8,128)(2,1)}, u32[]{:S(2)}) %copy-start.6) | copy-done | bytes 131096
  15.6 0.0 copy-start.9
  15.6 0.7 %copy-done.9 = f32[3,768]{1,0:T(4,128)S(1)} copy-done((f32[3,768]{1,0:T(4,128)S(1)}, f32[3,768]{1,0:T(4,128)}, u32[]{:S(2)}) %copy-start.9) | copy-done | bytes 9240
  16.3 0.0 copy-start.11
  16.3 0.7 %copy-done.11 = f32[256]{0:T(256)S(1)} copy-done((f32[256]{0:T(256)S(1)}, f32[256]{0:T(256)}, u32[]{:S(2)}) %copy-start.11) | copy-done | bytes 1048
  16.9 0.0 copy-start.1
  17.0 1.3 %shard_map.118 = (bf16[256,256]{1,0:T(8,128)(2,1)}, f32[256,256]{1,0:T(8,128)S(1)}) custom-call(bf16[256,256]{1,0:T(8,128)(2,1)S(1)} %copy-done.6, bf16[16,256]{1,0:T(8,128)(2,1)S(1)} %collective-permute-done.rim_ref, f32[1,256]{1,0:T(1,128)S(1)} %bitcast.13, bf16[256,768]{1,0:T(8,128)(2,1)S(1)} %copy-done.3, f32[3,768]{1,0:T(4,128)S(1)} %copy-done.9), custom_call_target="tpu_custom_call" | custom-call | flops 100663296 | bytes 1000000 | tf_op jit(solution)/shard_map/pallas_call | solution.py:23
  18.2 0.5 %all-to-all-done.1 = bf16[16,16,256]{2,1,0:T(8,128)(2,1)S(1)} async-done(((bf16[16,16,256]{2,1,0:T(8,128)(2,1)}), bf16[16,16,256]{2,1,0:T(8,128)(2,1)S(1)}, u32[]{:S(2)}, u32[]{:S(2)}) %all-to-all-start.1) | async-done | bytes 131104 | tf_op jit(solution)/shard_map/all_to_all | solution.py:150
  18.8 7.3 %all-to-all-start = ((bf16[16,16,256]{2,1,0:T(8,128)(2,1)}), bf16[16,16,256]{2,1,0:T(8,128)(2,1)S(1)}, u32[]{:S(2)}, u32[]{:S(2)}) async-start(bf16[16,16,256]{2,1,0:T(8,128)(2,1)} %bitcast.1), calls=%async_computation | async-start | bytes 262144 | tf_op jit(solution)/shard_map/all_to_all | solution.py:150
  26.1 0.0 copy-done.2
  26.1 0.0 copy-done
  26.1 0.0 copy-done.1
  26.1 0.0 copy-start.4
  26.1 0.6 %shard_map.120.spec_ref = f32[544,256]{1,0:T(8,128)S(1)} custom-call(bf16[256,256]{1,0:T(8,128)(2,1)S(1)} %bitcast.8, bf16[544,256]{1,0:T(8,128)(2,1)S(1)} %copy-done.1, f32[544,256]{1,0:T(8,128)S(1)} %copy-done, bf16[256,512]{1,0:T(8,128)(2,1)S(1)} %copy-done.2), custom_call_target="tpu_custom_call" | custom-call | flops 213909504 | bytes 1500000 | tf_op jit(solution)/shard_map/pallas_call | solution.py:23
  26.7 7.3 %all-to-all-done = bf16[16,16,256]{2,1,0:T(8,128)(2,1)S(1)} async-done(((bf16[16,16,256]{2,1,0:T(8,128)(2,1)}), bf16[16,16,256]{2,1,0:T(8,128)(2,1)S(1)}, u32[]{:S(2)}, u32[]{:S(2)}) %all-to-all-start) | async-done | bytes 131104 | tf_op jit(solution)/shard_map/all_to_all | solution.py:150
  34.0 0.0 copy-done.4
  34.0 1.3 %shard_map.121 = bf16[256,256]{1,0:T(8,128)(2,1)S(1)} custom-call(bf16[256,256]{1,0:T(8,128)(2,1)S(1)} %bitcast.9, f32[544,256]{1,0:T(8,128)S(1)} %shard_map.120.spec_ref, bf16[544,256]{1,0:T(8,128)(2,1)S(1)} %copy-done.1, f32[544,256]{1,0:T(8,128)S(1)} %copy-done, bf16[256,512]{1,0:T(8,128)(2,1)S(1)} %copy-done.2, bf16[256,544]{1,0:T(8,128)(2,1)S(1)} %copy-done.4), custom_call_target="tpu_custom_call" | custom-call | flops 427819008 | bytes 2000000 | tf_op jit(solution)/shard_map/pallas_call | solution.py:23
  35.3 0.0 copy-start.7
  35.3 10.7 %all_to_all.15 = bf16[16,16,256]{2,1,0:T(8,128)(2,1)S(1)} all-to-all(bf16[16,16,256]{2,1,0:T(8,128)(2,1)S(1)} %bitcast.10), channel_id=1, replica_groups=mesh['groups'=2,'seq'=16] {'seq'}, dimensions={0} | all-to-all | bytes 262144 | tf_op jit(solution)/shard_map/all_to_all | solution.py:150
  46.0 0.0 copy-done.7
  46.0 0.9 %shard_map.122 = bf16[256,256]{1,0:T(8,128)(2,1)} custom-call(bf16[256,256]{1,0:T(8,128)(2,1)S(1)} %bitcast.11, f32[256,256]{1,0:T(8,128)S(1)} %get-tuple-element.8.query_ref, bf16[256,256]{1,0:T(8,128)(2,1)S(1)} %copy-done.7), custom_call_target="tpu_custom_call" | custom-call | flops 33554432 | bytes 600000 | tf_op jit(solution)/shard_map/pallas_call | solution.py:23
Async XLA Ops:
  0.0 0.7 %copy-start.10 = (f32[256]{0:T(256)S(1)}, f32[256]{0:T(256)}, u32[]{:S(2)}) copy-start(f32[256]{0:T(256)} %param.18) | copy-start | bytes 3076
  0.7 0.9 %copy-start.5 = (f32[256,256]{1,0:T(8,128)S(1)}, f32[256,256]{1,0:T(8,128)}, u32[]{:S(2)}) copy-start(f32[256,256]{1,0:T(8,128)} %long_ref.1) | copy-start | bytes 786436
  1.6 0.9 %copy-start.8 = (f32[128,256]{1,0:T(8,128)S(1)}, f32[128,256]{1,0:T(8,128)}, u32[]{:S(2)}) copy-start(f32[128,256]{1,0:T(8,128)} %medium_ref.1) | copy-start | bytes 393220
  2.5 12.1 %copy-start.3 = (bf16[256,768]{1,0:T(8,128)(2,1)S(1)}, bf16[256,768]{1,0:T(8,128)(2,1)}, u32[]{:S(2)}) copy-start(bf16[256,768]{1,0:T(8,128)(2,1)} %w_ref.2) | copy-start | bytes 1179652
  2.5 23.6 %copy-start.2 = (bf16[256,512]{1,0:T(8,128)(2,1)S(1)}, bf16[256,512]{1,0:T(8,128)(2,1)}, u32[]{:S(2)}) copy-start(bf16[256,512]{1,0:T(8,128)(2,1)} %constant.10.clone.inner_ref) | copy-start | bytes 786436
  3.3 22.8 %copy-start = (f32[544,256]{1,0:T(8,128)S(1)}, f32[544,256]{1,0:T(8,128)}, u32[]{:S(2)}) copy-start(f32[544,256]{1,0:T(8,128)} %constant.9.clone.twist_ref) | copy-start | bytes 1671172
  3.3 15.5 %all-to-all-start.1 = ((bf16[16,16,256]{2,1,0:T(8,128)(2,1)}), bf16[16,16,256]{2,1,0:T(8,128)(2,1)S(1)}, u32[]{:S(2)}, u32[]{:S(2)}) async-start(bf16[16,16,256]{2,1,0:T(8,128)(2,1)} %bitcast.4), calls=%async_computation.1 | async-start | bytes 262144 | tf_op jit(solution)/shard_map/all_to_all | solution.py:150
  11.5 3.1 %collective-permute-start = (bf16[16,256]{1,0:T(8,128)(2,1)S(1)}, bf16[16,256]{1,0:T(8,128)(2,1)S(1)}, u32[]{:S(2)}, u32[]{:S(2)}) collective-permute-start(bf16[16,256]{1,0:T(8,128)(2,1)S(1)} %slice.3), channel_id=1, source_target_pairs={{0,1},{1,2},{2,3},{3,4},{4,5},{5,6},{6,7},{7,8},{8,9},{9,10},{10,1... | collective-permute-start | bytes 24584 | tf_op jit(solution)/shard_map/ppermute | solution.py:19
  14.7 0.9 %copy-start.6 = (bf16[256,256]{1,0:T(8,128)(2,1)S(1)}, bf16[256,256]{1,0:T(8,128)(2,1)}, u32[]{:S(2)}) copy-start(bf16[256,256]{1,0:T(8,128)(2,1)} %tokens_ref.1) | copy-start | bytes 393220
  15.6 0.7 %copy-start.9 = (f32[3,768]{1,0:T(4,128)S(1)}, f32[3,768]{1,0:T(4,128)}, u32[]{:S(2)}) copy-start(f32[3,768]{1,0:T(4,128)} %short_ref.1) | copy-start | bytes 27652
  16.3 0.7 %copy-start.11 = (f32[256]{0:T(256)S(1)}, f32[256]{0:T(256)}, u32[]{:S(2)}) copy-start(f32[256]{0:T(256)} %param.13) | copy-start | bytes 3076
  16.9 9.2 %copy-start.1 = (bf16[544,256]{1,0:T(8,128)(2,1)S(1)}, bf16[544,256]{1,0:T(8,128)(2,1)}, u32[]{:S(2)}) copy-start(bf16[544,256]{1,0:T(8,128)(2,1)} %constant.8.clone.first_ref) | copy-start | bytes 835588
  18.8 15.3 %all-to-all-start = ((bf16[16,16,256]{2,1,0:T(8,128)(2,1)}), bf16[16,16,256]{2,1,0:T(8,128)(2,1)S(1)}, u32[]{:S(2)}, u32[]{:S(2)}) async-start(bf16[16,16,256]{2,1,0:T(8,128)(2,1)} %bitcast.1), calls=%async_computation | async-start | bytes 262144 | tf_op jit(solution)/shard_map/all_to_all | solution.py:150
  26.1 7.9 %copy-start.4 = (bf16[256,544]{1,0:T(8,128)(2,1)S(1)}, bf16[256,544]{1,0:T(8,128)(2,1)}, u32[]{:S(2)}) copy-start(bf16[256,544]{1,0:T(8,128)(2,1)} %constant.11.clone.last_ref) | copy-start | bytes 835588
  35.3 10.7 %copy-start.7 = (bf16[256,256]{1,0:T(8,128)(2,1)S(1)}, bf16[256,256]{1,0:T(8,128)(2,1)}, u32[]{:S(2)}) copy-start(bf16[256,256]{1,0:T(8,128)(2,1)} %w_ref.3) | copy-start | bytes 393220
